TPU v7x, 32 devices: a whole 2x2x4 slice. The times are simulated.
32 devices in a mesh: dp: 16 (over z, x, core), tensor: 2 (over y).
Axes of the slice: x: 2, y: 2, z: 4, core: 2. Of those that a mesh axis runs over, the one named last changes fastest.
Arguments:
- tokens: bfloat16 [32, 1024, 768], P('dp', 'tensor'), may hold values from -6 to 6
- lengths: int32 [32], P('dp'), may hold values from 128 to 1024, as said below
- layer_index: int32 [1], replicated, may hold values from 0 to 3
- norm_one_gain: bfloat16 [4, 768], replicated, may hold values from 0.5 to 1.5
- norm_one_bias: bfloat16 [4, 768], replicated, may hold values from -1.1953125 to 1.1953125
- attend_weight: bfloat16 [4, 768, 3, 768], P(None, None, None, 'tensor'), may hold values from -0.21875 to 0.21875
- query_bias: bfloat16 [4, 768], P(None, 'tensor'), may hold values from -1.1953125 to 1.1953125
- value_bias: bfloat16 [4, 768], P(None, 'tensor'), may hold values from -1.1953125 to 1.1953125
- output_weight: bfloat16 [4, 768, 768], P(None, 'tensor'), may hold values from -0.875 to 0.875
- output_bias: bfloat16 [4, 768], replicated, may hold values from -1.1953125 to 1.1953125
- norm_two_gain: bfloat16 [4, 768], replicated, may hold values from 0.5 to 1.5
- norm_two_bias: bfloat16 [4, 768], replicated, may hold values from -1.1953125 to 1.1953125
- expand_weight: bfloat16 [4, 768, 3072], P(None, None, 'tensor'), may hold values from -0.21875 to 0.21875
- expand_bias: bfloat16 [4, 3072], P(None, 'tensor'), may hold values from -1.1953125 to 1.1953125
- shrink_weight: bfloat16 [4, 3072, 768], P(None, 'tensor'), may hold values from -0.109375 to 0.109375
- shrink_bias: bfloat16 [4, 768], replicated, may hold values from -1.1953125 to 1.1953125
- cotangent: bfloat16 [32, 1024, 768], P('dp', 'tensor'), may hold values from -6 to 6
Outputs:
- block_output: float32 [32, 1024, 768], P('dp', 'tensor')
- input_grad: float32 [32, 1024, 768], P('dp', 'tensor')
- norm_one_gain_grad: float32 [768], replicated
- norm_one_bias_grad: float32 [768], replicated
- attend_weight_grad: float32 [768, 3, 768], P(None, None, 'tensor')
- query_bias_grad: float32 [768], P('tensor')
- value_bias_grad: float32 [768], P('tensor')
- output_weight_grad: float32 [768, 768], P('tensor')
- output_bias_grad: float32 [768], replicated
- norm_two_gain_grad: float32 [768], replicated
- norm_two_bias_grad: float32 [768], replicated
- expand_weight_grad: float32 [768, 3072], P(None, 'tensor')
- expand_bias_grad: float32 [3072], P('tensor')
- shrink_weight_grad: float32 [3072, 768], P('tensor')
- shrink_bias_grad: float32 [768], replicated
- rms_values: float32 [3], replicated
Inputs may be any that keep to these rules, and one draw needn't show every extreme that they name: `lengths`: of the 2 sequences of each aligned block, one is longer than 512; some sequence has exactly 1024 tokens.
All inputs are finite; a program needn't handle non-finite values.
Results may differ from a plain program's by a relative error of at most 0.011.
Values may be sent and summed in bfloat16 or wider, within the bound.
A program may use at most 256 MiB of HBM per device.

v0:
```python
import jax
import jax.numpy as jnp
from jax import lax
from jax.sharding import PartitionSpec as P

HD = 64


epsilon = 1e-05
masked_fill = -1e30


def layer_norm(values, gain, shift):
    center = jnp.mean(values, axis=-1, keepdims=True)
    centered = values - center
    spread = jnp.mean(centered * centered, axis=-1, keepdims=True)
    return centered * lax.rsqrt(spread + epsilon) * gain + shift


def gelu_tanh(values):
    return jax.nn.gelu(values, approximate=True)


def select_layer(stack, layer_index):
    return lax.dynamic_index_in_dim(stack, layer_index[0], 0, keepdims=False)


def outer_sum(left, right):
    return lax.dot_general(
        left, right, (((0,), (0,)), ((), ())), preferred_element_type=jnp.float32
    )


def back_product(left, right):
    return lax.dot_general(
        left, right, (((1,), (1,)), ((), ())), preferred_element_type=jnp.float32
    )


def block_scores(query, key, lengths, index, block, scale):
    keys_end = (index + 1) * block
    rows = query[:, index * block : keys_end]
    raw = jnp.einsum("sqhd,skhd->shqk", rows, key[:, :keys_end], preferred_element_type=jnp.float32)
    query_pos = index * block + lax.broadcasted_iota(jnp.int32, (block, keys_end), 0)
    key_pos = lax.broadcasted_iota(jnp.int32, (block, keys_end), 1)
    allowed = (key_pos <= query_pos)[None, None] & (
        key_pos[None, None] < lengths[:, None, None, None]
    )
    return jnp.where(allowed, raw * scale, masked_fill)


def attention_forward(query, key, value, lengths):
    seq_len = query.shape[1]
    block = min(512, seq_len)
    scale = query.shape[3] ** (-0.5)
    outputs = []
    maxima = []
    for index in range(seq_len // block):
        keys_end = (index + 1) * block
        scores = block_scores(query, key, lengths, index, block, scale)
        top = jnp.max(scores, axis=-1, keepdims=True)
        weights = jnp.exp(scores - top)
        total = jnp.sum(weights, axis=-1, keepdims=True)
        shares = (weights / total).astype(jnp.bfloat16)
        outputs.append(
            jnp.einsum(
                "shqk,skhd->sqhd", shares, value[:, :keys_end], preferred_element_type=jnp.float32
            )
        )
        maxima.append(top + jnp.log(total))
    return (jnp.concatenate(outputs, axis=1), jnp.concatenate(maxima, axis=2))


def attention_backward(query, key, value, maxima, grad_mixed, lengths):
    seq_len = query.shape[1]
    block = min(512, seq_len)
    scale = query.shape[3] ** (-0.5)
    grad_query = []
    grad_key = jnp.zeros(key.shape, jnp.float32)
    grad_value = jnp.zeros(value.shape, jnp.float32)
    for index in range(seq_len // block):
        keys_end = (index + 1) * block
        scores = block_scores(query, key, lengths, index, block, scale)
        shares = jnp.exp(scores - maxima[:, :, index * block : keys_end])
        grad_rows = grad_mixed[:, index * block : keys_end]
        query_rows = query[:, index * block : keys_end]
        grad_shares = jnp.einsum(
            "sqhd,skhd->shqk", grad_rows, value[:, :keys_end], preferred_element_type=jnp.float32
        )
        inner = jnp.sum(shares * grad_shares, axis=-1, keepdims=True)
        grad_scores = (shares * (grad_shares - inner)).astype(jnp.bfloat16)
        grad_query.append(
            jnp.einsum(
                "shqk,skhd->sqhd",
                grad_scores,
                key[:, :keys_end],
                preferred_element_type=jnp.float32,
            )
            * scale
        )
        grad_key = grad_key.at[:, :keys_end].add(
            jnp.einsum(
                "shqk,sqhd->skhd", grad_scores, query_rows, preferred_element_type=jnp.float32
            )
            * scale
        )
        grad_value = grad_value.at[:, :keys_end].add(
            jnp.einsum(
                "shqk,sqhd->skhd",
                shares.astype(jnp.bfloat16),
                grad_rows,
                preferred_element_type=jnp.float32,
            )
        )
    return (jnp.concatenate(grad_query, axis=1), grad_key, grad_value)


def body(
    tokens,
    lengths,
    layer_index,
    norm_one_gain,
    norm_one_bias,
    attend_weight,
    query_bias,
    value_bias,
    output_weight,
    output_bias,
    norm_two_gain,
    norm_two_bias,
    expand_weight,
    expand_bias,
    shrink_weight,
    shrink_bias,
    cotangent,
):
    seq_dev, half_len, width = tokens.shape
    seq_len = half_len * lax.axis_size("tensor")
    first_row = lax.axis_index("tensor") * half_len
    positions = first_row + lax.broadcasted_iota(jnp.int32, (seq_dev, half_len), 1)
    valid = (positions < lengths[:, None]).astype(jnp.float32).reshape(-1, 1)
    gain_one = select_layer(norm_one_gain, layer_index).astype(jnp.float32)
    shift_one = select_layer(norm_one_bias, layer_index).astype(jnp.float32)
    attend_flat = select_layer(attend_weight, layer_index).reshape(width, -1)
    local_width = attend_flat.shape[1] // 3
    heads = local_width // HD
    query_shift = select_layer(query_bias, layer_index).astype(jnp.float32)
    value_shift = select_layer(value_bias, layer_index).astype(jnp.float32)
    out_mat = select_layer(output_weight, layer_index)
    out_shift = select_layer(output_bias, layer_index).astype(jnp.float32)
    gain_two = select_layer(norm_two_gain, layer_index).astype(jnp.float32)
    shift_two = select_layer(norm_two_bias, layer_index).astype(jnp.float32)
    expand_mat = select_layer(expand_weight, layer_index)
    expand_shift = select_layer(expand_bias, layer_index).astype(jnp.float32)
    shrink_mat = select_layer(shrink_weight, layer_index)
    shrink_shift = select_layer(shrink_bias, layer_index).astype(jnp.float32)

    def masked_norm(values, gain, shift):
        return valid * layer_norm(values, gain, shift)

    row_shape = (seq_dev, half_len, width)
    full_shape = (seq_dev, seq_len, width)
    rows_in = tokens.astype(jnp.float32).reshape(-1, width)
    normed_one, norm_one_back = jax.vjp(masked_norm, rows_in, gain_one, shift_one)
    normed_full = lax.all_gather(
        normed_one.astype(jnp.bfloat16).reshape(row_shape), "tensor", axis=1, tiled=True
    ).reshape(-1, width)
    projected = jnp.dot(normed_full, attend_flat, preferred_element_type=jnp.float32).reshape(
        -1, 3, local_width
    )
    head_shape = (seq_dev, seq_len, heads, HD)
    query = (projected[:, 0] + query_shift).astype(jnp.bfloat16).reshape(head_shape)
    key = projected[:, 1].astype(jnp.bfloat16).reshape(head_shape)
    value = (projected[:, 2] + value_shift).astype(jnp.bfloat16).reshape(head_shape)
    attended, maxima = attention_forward(query, key, value, lengths)
    mixed = attended.astype(jnp.bfloat16).reshape(-1, local_width)
    partial_attn = jnp.dot(mixed, out_mat, preferred_element_type=jnp.float32).reshape(full_shape)
    attn_rows = (
        lax.psum_scatter(partial_attn, "tensor", scatter_dimension=1, tiled=True).reshape(-1, width)
        + out_shift
    )
    resid_one = rows_in + valid * attn_rows
    normed_two, norm_two_back = jax.vjp(masked_norm, resid_one, gain_two, shift_two)
    hidden_in = lax.all_gather(
        normed_two.astype(jnp.bfloat16).reshape(row_shape), "tensor", axis=1, tiled=True
    ).reshape(-1, width)
    pre_act = jnp.dot(hidden_in, expand_mat, preferred_element_type=jnp.float32) + expand_shift
    activated, gelu_back = jax.vjp(gelu_tanh, pre_act)
    act_low = activated.astype(jnp.bfloat16)
    partial_mlp = jnp.dot(act_low, shrink_mat, preferred_element_type=jnp.float32).reshape(
        full_shape
    )
    mlp_rows = (
        lax.psum_scatter(partial_mlp, "tensor", scatter_dimension=1, tiled=True).reshape(-1, width)
        + shrink_shift
    )
    result = resid_one + valid * mlp_rows
    grad_out = cotangent.astype(jnp.float32).reshape(-1, width)
    grad_mlp = valid * grad_out
    shrink_shift_grad = jnp.sum(grad_mlp, axis=0)
    grad_mlp_full = lax.all_gather(
        grad_mlp.astype(jnp.bfloat16).reshape(row_shape), "tensor", axis=1, tiled=True
    ).reshape(-1, width)
    shrink_mat_grad = outer_sum(act_low, grad_mlp_full)
    grad_act = back_product(grad_mlp_full, shrink_mat)
    grad_pre = gelu_back(grad_act)[0].astype(jnp.bfloat16)
    expand_shift_grad = jnp.sum(grad_pre.astype(jnp.float32), axis=0)
    expand_mat_grad = outer_sum(hidden_in, grad_pre)
    grad_hidden = back_product(grad_pre, expand_mat).reshape(full_shape)
    grad_normed_two = lax.psum_scatter(
        grad_hidden, "tensor", scatter_dimension=1, tiled=True
    ).reshape(-1, width)
    grad_resid, gain_two_grad, shift_two_grad = norm_two_back(grad_normed_two)
    grad_resid = grad_out + grad_resid
    grad_attn = valid * grad_resid
    out_shift_grad = jnp.sum(grad_attn, axis=0)
    grad_attn_full = lax.all_gather(
        grad_attn.astype(jnp.bfloat16).reshape(row_shape), "tensor", axis=1, tiled=True
    ).reshape(-1, width)
    out_mat_grad = outer_sum(mixed, grad_attn_full)
    grad_mixed = back_product(grad_attn_full, out_mat).astype(jnp.bfloat16).reshape(head_shape)
    grad_query, grad_key, grad_value = attention_backward(
        query, key, value, maxima, grad_mixed, lengths
    )
    grad_query = grad_query.astype(jnp.bfloat16).reshape(-1, local_width)
    grad_key = grad_key.astype(jnp.bfloat16).reshape(-1, local_width)
    grad_value = grad_value.astype(jnp.bfloat16).reshape(-1, local_width)
    query_shift_grad = jnp.sum(grad_query.astype(jnp.float32), axis=0)
    value_shift_grad = jnp.sum(grad_value.astype(jnp.float32), axis=0)
    grad_stack = jnp.stack([grad_query, grad_key, grad_value], axis=1).reshape(-1, 3 * local_width)
    attend_grad = outer_sum(normed_full, grad_stack).reshape(width, 3, local_width)
    grad_normed = back_product(grad_stack, attend_flat).reshape(full_shape)
    grad_normed_one = lax.psum_scatter(
        grad_normed, "tensor", scatter_dimension=1, tiled=True
    ).reshape(-1, width)
    grad_input, gain_one_grad, shift_one_grad = norm_one_back(grad_normed_one)
    grad_input = grad_resid + grad_input
    summed = lax.psum(
        (
            attend_grad,
            query_shift_grad,
            value_shift_grad,
            out_mat_grad,
            expand_mat_grad,
            expand_shift_grad,
            shrink_mat_grad,
        ),
        "dp",
    )
    attend_grad, query_shift_grad, value_shift_grad, out_mat_grad = (
        summed[0],
        summed[1],
        summed[2],
        summed[3],
    )
    expand_mat_grad, expand_shift_grad, shrink_mat_grad = (summed[4], summed[5], summed[6])
    counters = jnp.stack(
        [
            jnp.sum(valid * result * result),
            jnp.sum(valid * attn_rows * attn_rows),
            jnp.sum(valid * mlp_rows * mlp_rows),
            jnp.sum(valid),
        ]
    )
    small = lax.psum(
        (
            gain_one_grad,
            shift_one_grad,
            out_shift_grad,
            gain_two_grad,
            shift_two_grad,
            shrink_shift_grad,
            counters,
        ),
        ("dp", "tensor"),
    )
    totals = small[6]
    rms_values = jnp.sqrt(totals[:3] / (totals[3] * width))
    return (
        result.reshape(row_shape),
        grad_input.reshape(row_shape),
        small[0],
        small[1],
        attend_grad,
        query_shift_grad,
        value_shift_grad,
        out_mat_grad,
        small[2],
        small[3],
        small[4],
        expand_mat_grad,
        expand_shift_grad,
        shrink_mat_grad,
        small[5],
        rms_values,
    )


def solution(mesh):
    in_specs = (
        P("dp", "tensor", None),
        P("dp"),
        P(),
        P(),
        P(),
        P(None, None, None, "tensor"),
        P(None, "tensor"),
        P(None, "tensor"),
        P(None, "tensor", None),
        P(),
        P(),
        P(),
        P(None, None, "tensor"),
        P(None, "tensor"),
        P(None, "tensor", None),
        P(),
        P("dp", "tensor", None),
    )
    out_specs = (
        P("dp", "tensor", None),
        P("dp", "tensor", None),
        P(),
        P(),
        P(None, None, "tensor"),
        P("tensor"),
        P("tensor"),
        P("tensor", None),
        P(),
        P(),
        P(),
        P(None, "tensor"),
        P("tensor"),
        P("tensor", None),
        P(),
        P(),
    )
    return jax.shard_map(body, mesh=mesh, in_specs=in_specs, out_specs=out_specs, check_vma=False)
```

profile of v0, /device:TPU:0, one launch (start us, length us, event | category | flops | bytes accessed | tf_op | source)
XLA Modules:
  0.0 1006.0 jit_solution(6655548631018318025)
XLA Ops:
  26.3 38.4 %all-gather.5.cloned.1.call-done = bf16[2,1024,768]{2,1,0:T(8,128)(2,1)} async-done(((bf16[2,512,768]{2,1,0:T(8,128)(2,1)}), bf16[2,1024,768]{2,1,0:T(8,128)(2,1)}) %all-gather.5.cloned.1.call-update) | async-done | bytes 3145744 | tf_op jit(solution)/shard_map/all_gather | solution.py:165
  121.6 12.3 %fusion.121 = (f32[2,6,512]{2,1,0:T(8,128)S(1)}, f32[2,6,512,1024]{3,2,1,0:T(8,128)}) fusion(bf16[2,1024,6,64]{1,0,3,2:T(2,128)(2,1)} %convert_element_type.139, bf16[2,1024,6,64]{1,3,2,0:T(8,128)(2,1)} %copy-done.12, pred[2,512,1024]{2,1,0:T(8,128)(4,1)S(1)} %fusion.27), kind=kOutput, calls=%fused_computation.196 | convolution fusion | flops 824174592 | bytes 28598272 | tf_op jit(solution)/shard_map/sqhd,skhd->shqk/dot_general | solution.py:43
  134.0 11.1 %fusion = f32[2,6,512]{2,1,0:T(8,128)S(1)} fusion(f32[2,6,512,1024]{3,2,1,0:T(8,128)} %get-tuple-element.121, f32[2,6,512]{2,1,0:T(8,128)S(1)} %get-tuple-element.120), kind=kLoop, calls=%fused_computation.6 | loop fusion | flops 12576768 | bytes 25214976 | tf_op jit(solution)/shard_map/reduce_sum | solution.py:63
  145.0 11.4 %fusion.69 = bf16[2,6,64,512]{3,2,1,0:T(8,128)(2,1)} fusion(bf16[2,1024,6,64]{1,3,2,0:T(8,128)(2,1)S(1)} %copy-done.17, f32[2,6,512,1024]{3,2,1,0:T(8,128)} %get-tuple-element.121, f32[2,6,512]{2,1,0:T(8,128)S(1)} %fusion, f32[2,6,512]{2,1,0:T(8,128)S(1)} %get-tuple-element.120), kind=kOutput, calls=%fused_computation.115 | convolution fusion | flops 824573952 | bytes 27574272 | tf_op jit(solution)/shard_map/shqk,skhd->sqhd/dot_general | solution.py:66
  165.1 76.5 %reduce-scatter.5.cloned.1.call-done = f32[2,512,768]{2,1,0:T(8,128)} async-done(((f32[2,1024,768]{2,1,0:T(8,128)}), f32[2,512,768]{2,1,0:T(8,128)}) %reduce-scatter.5.cloned.1.call-update) | async-done | bytes 3145744 | tf_op jit(solution)/shard_map/reduce_scatter | solution.py:179
  251.2 44.4 %all-gather.7.cloned.1.call-done = bf16[2,1024,768]{2,1,0:T(8,128)(2,1)} async-done(((bf16[2,512,768]{2,1,0:T(8,128)(2,1)}), bf16[2,1024,768]{2,1,0:T(8,128)(2,1)}) %all-gather.7.cloned.1.call-update) | async-done | bytes 3145744 | tf_op jit(solution)/shard_map/all_gather | solution.py:184
  295.6 13.7 %multiply_convert_fusion.2 = (bf16[2048,1536]{1,0:T(8,128)(2,1)}, f32[2048,1536]{1,0:T(8,128)}) fusion(f32[1536]{0:T(1024)S(1)} %convert_reduce_fusion.4, bf16[2048,768]{1,0:T(8,128)(2,1)} %bitcast.132, bf16[4,768,1536]{2,1,0:T(8,128)(2,1)} %param.41, s32[]{:T(128)S(6)} %select_n.32), kind=kOutput, calls=%fused_computation.23 | convolution fusion | flops 4863295488 | bytes 24385540 | tf_op jit(solution)/shard_map/dot_general | solution.py:187
  309.3 32.7 %all-gather.9.cloned.1.call-done = bf16[2,1024,768]{2,1,0:T(8,128)(2,1)} async-done(((bf16[2,512,768]{2,1,0:T(8,128)(2,1)}), bf16[2,1024,768]{2,1,0:T(8,128)(2,1)}) %all-gather.9.cloned.1.call-update) | async-done | bytes 3145744 | tf_op jit(solution)/shard_map/all_gather | solution.py:201
  342.1 17.2 %convert_reduce_fusion = (f32[1536]{0:T(1024)}, bf16[2048,1536]{1,0:T(8,128)(2,1)S(1)}) fusion(f32[2048,1536]{1,0:T(8,128)} %get-tuple-element.125, f32[1536]{0:T(1024)S(1)} %convert_reduce_fusion.4, bf16[2048,768]{1,0:T(8,128)(2,1)} %bitcast.134, bf16[4,1536,768]{2,1,0:T(8,128)(2,1)} %param.43, s32[]{:T(128)S(6)} %select_n.32), kind=kOutput, calls=%fused_computation.18 | convolution fusion | flops 4904188416 | bytes 24391684 | tf_op jit(solution)/shard_map/dot_general | solution.py:35
  361.9 8.6 fusion.45
  371.0 76.8 %reduce-scatter.9.cloned.1.call-done = f32[2,512,768]{2,1,0:T(8,128)} async-done(((f32[2,1024,768]{2,1,0:T(8,128)}), f32[2,512,768]{2,1,0:T(8,128)}) %reduce-scatter.9.cloned.1.call-update) | async-done | bytes 3145744 | tf_op jit(solution)/shard_map/reduce_scatter | solution.py:210
  457.1 9.5 fusion.47
  466.7 35.4 %all-gather.11.cloned.1.call-done = bf16[2,1024,768]{2,1,0:T(8,128)(2,1)} async-done(((bf16[2,512,768]{2,1,0:T(8,128)(2,1)}), bf16[2,1024,768]{2,1,0:T(8,128)(2,1)}) %all-gather.11.cloned.1.call-update) | async-done | bytes 3145744 | tf_op jit(solution)/shard_map/all_gather | solution.py:217
  520.7 11.0 %convert_reduce_fusion.2 = (f32[6,64]{1,0:T(8,128)S(1)}, bf16[2,1024,6,64]{1,3,2,0:T(8,128)(2,1)S(1)}) fusion(f32[2,6,512,1024]{3,2,1,0:T(8,128)} %get-tuple-element.121, f32[2,6,512]{2,1,0:T(8,128)S(1)} %log_add_fusion, bf16[2,512,6,64]{1,0,3,2:T(2,128)(2,1)S(1)} %get-tuple-element.118, f32[2,512,6,64]{1,3,2,0:T(8,128)S(1)} %fusion.65), kind=kOutput, calls=%fused_computation.78 | convolution fusion | flops 821034624 | bytes 29124096 | tf_op jit(solution)/shard_map/shqk,sqhd->skhd/dot_general | solution.py:108
  557.7 18.3 %multiply_reduce_fusion = (f32[2,6,512]{2,1,0:T(8,128)S(1)}, f32[2,6,512,1024]{3,2,1,0:T(8,128)}) fusion(f32[2,6,512,1024]{3,2,1,0:T(8,128)} %get-tuple-element.121, f32[2,6,512]{2,1,0:T(8,128)S(1)} %log_add_fusion, bf16[2,1024,6,64]{1,3,2,0:T(8,128)(2,1)} %copy-done.16, bf16[2,512,6,64]{1,0,3,2:T(2,128)(2,1)S(1)} %get-tuple-element.118), kind=kOutput, calls=%fused_computation.1 | convolution fusion | flops 824174592 | bytes 52740096 | tf_op jit(solution)/shard_map/sqhd,skhd->shqk/dot_general | solution.py:87
  576.0 16.7 %multiply_convert_fusion = bf16[2,6,512,1024]{3,2,1,0:T(8,128)(2,1)S(1)} fusion(f32[2,6,512,1024]{3,2,1,0:T(8,128)} %get-tuple-element.127, f32[2,6,512,1024]{3,2,1,0:T(8,128)} %get-tuple-element.121, f32[2,6,512]{2,1,0:T(8,128)S(1)} %get-tuple-element.126, f32[2,6,512]{2,1,0:T(8,128)S(1)} %log_add_fusion), kind=kLoop, calls=%fused_computation | loop fusion | flops 25165824 | bytes 62963712 | tf_op jit(solution)/shard_map/convert_element_type | solution.py:91
  605.6 8.5 multiply_bitcast_fusion.1
  626.5 8.9 dot_general.111
  635.4 10.3 %fusion.25 = f32[2,1024,768]{2,1,0:T(8,128)} fusion(bf16[768,1152,1]{0,1,2:T(8,128)(2,1)S(1)} %bitcast.128, bf16[2,1024,1152]{1,0,2:T(2,128)(2,1)} %dot_general.111), kind=kOutput, calls=%fused_computation.45 | convolution fusion | flops 3623878656 | bytes 12779520 | tf_op jit(solution)/shard_map/dot_general | solution.py:35
  649.4 10.7 %fusion.124 = f32[768,1536]{1,0:T(8,128)} fusion(bf16[2048,768]{1,0:T(8,128)(2,1)S(1)} %bitcast.133, bf16[2048,1536]{1,0:T(8,128)(2,1)} %copy-done.63), kind=kOutput, calls=%fused_computation.199 | convolution fusion | flops 4831838208 | bytes 14155776 | tf_op jit(solution)/shard_map/dot_general | solution.py:29
  679.6 60.8 %all-reduce.3 = (f32[384]{0:T(512)}, f32[384]{0:T(512)}, f32[1536]{0:T(1024)}) all-reduce(f32[384]{0:T(512)S(1)} %reduce_sum.276, f32[384]{0:T(512)S(1)} %reduce_sum.278, f32[1536]{0:T(1024)S(1)} %copy-done.47), channel_id=1, replica_groups=mesh['dp'=16,'tensor'=2] {'dp'}, use_global_device_ids=true, to_apply=%region_24.25 | all-reduce | flops 2304 | bytes 18432 | tf_op jit(solution)/shard_map/psum | solution.py:238
  740.5 9.9 fusion.40
  755.1 39.0 %all-reduce.2 = (f32[768]{0:T(1024)}, f32[768]{0:T(1024)}, f32[768]{0:T(1024)}, f32[768]{0:T(1024)}, f32[768]{0:T(1024)}, /*index=5*/f32[768]{0:T(1024)}, f32[4]{0:T(128)S(1)}) all-reduce(f32[768]{0:T(1024)S(1)} %get-tuple-element.82, f32[768]{0:T(1024)S(1)} %get-tuple-element.85, ...), channel_id=1, replica_groups=mesh['dp'=16,'tensor'=2] {'dp','tensor'}, use_global_device_ids=true, to_apply=%region_19.20 | all-reduce | flops 4612 | bytes 36896 | tf_op jit(solution)/shard_map/psum | solution.py:265
  801.1 187.3 %all-reduce.7.cloned.1.call-done = (f32[768,3,384]{2,0,1:T(8,128)}, f32[384,768]{1,0:T(8,128)}, f32[768,1536]{1,0:T(8,128)}, f32[1536,768]{1,0:T(8,128)}) async-done(((f32[768,3,384]{2,0,1:T(8,128)}, f32[384,768]{1,0:T(8,128)}, f32[768,1536]{1,0:T(8,128)}, f32[1536,768]{1,0:T(8,128)}), (f32[768,3,384]{2,0,1:T(8,128)}, f32[384,768]{1,0:T(8,128)}, f32[768,1536]{1,0:T(8,128)}, ...) | async-done | bytes 14155792 | tf_op jit(solution)/shard_map/psum | solution.py:238
  (255 shorter events, 220.1 us)
Async XLA Ops:
  7.2 151.5 %copy-start = (bf16[4,384,768]{2,1,0:T(8,128)(2,1)S(1)}, bf16[4,384,768]{2,1,0:T(8,128)(2,1)}, u32[]{:S(2)}) copy-start(bf16[4,384,768]{2,1,0:T(8,128)(2,1)} %param.37) | copy-start | bytes 7077892
  7.2 57.5 %all-gather.5.cloned.1.call-start = ((), (), s32[]{:S(2)}) async-start(), calls=%async_computation.4 | async-start | bytes 4718592 | tf_op jit(solution)/shard_map/all_gather | solution.py:165
  12.0 441.8 %copy-start.29 = (f32[2,512]{1,0:T(2,128)}, f32[2,512]{1,0:T(2,128)S(1)}, u32[]{:S(2)}) copy-start(f32[2,512]{1,0:T(2,128)S(1)} %compare_convert_fusion) | copy-start | bytes 12292
  16.9 224.6 %reduce-scatter.5.cloned.1.call-start = ((), (), s32[]{:S(2)}) async-start(), calls=%async_computation.5 | async-start | bytes 9437184 | tf_op jit(solution)/shard_map/reduce_scatter | solution.py:179
  145.0 13.7 %copy-start.23 = (bf16[2,512,384]{2,1,0:T(8,128)(2,1)S(1)}, bf16[2,512,384]{2,1,0:T(8,128)(2,1)}, u32[]{:S(2)}) copy-start(bf16[2,512,384]{2,1,0:T(8,128)(2,1)} %copy.59) | copy-start | bytes 2359300
  164.3 131.3 %all-gather.7.cloned.1.call-start = ((), (), s32[]{:S(2)}) async-start(), calls=%async_computation.6 | async-start | bytes 4718592 | tf_op jit(solution)/shard_map/all_gather | solution.py:184
  165.0 81.3 %copy-start.41 = (f32[768]{0:T(1024)}, f32[768]{0:T(1024)S(1)}, u32[]{:S(2)}) copy-start(f32[768]{0:T(1024)S(1)} %get-tuple-element.136) | copy-start | bytes 9220
  250.5 91.5 %all-gather.9.cloned.1.call-start = ((), (), s32[]{:S(2)}) async-start(), calls=%async_computation.8 | async-start | bytes 4718592 | tf_op jit(solution)/shard_map/all_gather | solution.py:201
  251.1 196.6 %reduce-scatter.9.cloned.1.call-start = ((), (), s32[]{:S(2)}) async-start(), calls=%async_computation.9 | async-start | bytes 9437184 | tf_op jit(solution)/shard_map/reduce_scatter | solution.py:210
  370.5 131.6 %all-gather.11.cloned.1.call-start = ((), (), s32[]{:S(2)}) async-start(), calls=%async_computation.10 | async-start | bytes 4718592 | tf_op jit(solution)/shard_map/all_gather | solution.py:217
  457.0 283.4 %reduce-scatter.7.cloned.1.call-start = ((), (), s32[]{:S(2)}) async-start(), calls=%async_computation.7 | async-start | bytes 9437184 | tf_op jit(solution)/shard_map/reduce_scatter | solution.py:194
  466.7 273.8 %reduce-scatter.11.cloned.1.call-start = ((), (), s32[]{:S(2)}) async-start(), calls=%async_computation.11 | async-start | bytes 9437184 | tf_op jit(solution)/shard_map/reduce_scatter | solution.py:233
  576.0 16.8 %copy-start.21 = (f32[2,512,6,64]{1,3,2,0:T(8,128)S(1)}, f32[2,512,6,64]{1,3,2,0:T(8,128)}, u32[]{:S(2)}) copy-start(f32[2,512,6,64]{1,3,2,0:T(8,128)} %multiply_bitcast_fusion) | copy-start | bytes 4718596
  645.8 342.6 %all-reduce.7.cloned.1.call-start = ((), (), s32[]{:S(2)}) async-start(), calls=%async_computation.12 | async-start | bytes 28311552 | tf_op jit(solution)/shard_map/psum | solution.py:238
  647.3 12.9 %slice-start.4 = ((s8[6291456]{0:T(1024)(128)(4,1)}), s8[4194304]{0:T(1024)(128)(4,1)S(1)}, s32[]{:S(2)}) async-start(s8[6291456]{0:T(1024)(128)(4,1)} %bitcast.139), calls=%async_computation.17 | async-start | bytes 8388608
  678.0 62.4 %copy-start.6 = (bf16[2,512,768]{2,1,0:T(8,128)(2,1)S(1)}, bf16[2,512,768]{2,1,0:T(8,128)(2,1)}, u32[]{:S(2)}) copy-start(bf16[2,512,768]{2,1,0:T(8,128)(2,1)} %param.29) | copy-start | bytes 4718596
  678.1 62.4 %copy-start.30 = (f32[2,512]{1,0:T(2,128)S(1)}, f32[2,512]{1,0:T(2,128)}, u32[]{:S(2)}) copy-start(f32[2,512]{1,0:T(2,128)} %copy-done.29) | copy-start | bytes 12292
  678.1 62.4 %copy-start.32 = (f32[2,512]{1,0:T(2,128)S(1)}, f32[2,512]{1,0:T(2,128)}, u32[]{:S(2)}) copy-start(f32[2,512]{1,0:T(2,128)} %copy-done.31) | copy-start | bytes 12292
  678.1 62.4 %copy-start.34 = (f32[768]{0:T(1024)S(1)}, f32[768]{0:T(1024)}, u32[]{:S(2)}) copy-start(f32[768]{0:T(1024)} %copy-done.33) | copy-start | bytes 9220
  678.1 62.4 %copy-start.38 = (f32[2,512]{1,0:T(2,128)S(1)}, f32[2,512]{1,0:T(2,128)}, u32[]{:S(2)}) copy-start(f32[2,512]{1,0:T(2,128)} %copy-done.37) | copy-start | bytes 12292
  678.1 62.4 %copy-start.42 = (f32[768]{0:T(1024)S(1)}, f32[768]{0:T(1024)}, u32[]{:S(2)}) copy-start(f32[768]{0:T(1024)} %copy-done.41) | copy-start | bytes 9220
  740.4 12.7 %copy-start.40 = (f32[2,512]{1,0:T(2,128)S(1)}, f32[2,512]{1,0:T(2,128)}, u32[]{:S(2)}) copy-start(f32[2,512]{1,0:T(2,128)} %copy-done.39) | copy-start | bytes 12292
  740.4 12.7 %copy-start.36 = (f32[2,512]{1,0:T(2,128)S(1)}, f32[2,512]{1,0:T(2,128)}, u32[]{:S(2)}) copy-start(f32[2,512]{1,0:T(2,128)} %copy-done.35) | copy-start | bytes 12292
  740.5 12.6 %copy-start.9 = (f32[2,512,768]{2,1,0:T(8,128)S(1)}, f32[2,512,768]{2,1,0:T(8,128)}, u32[]{:S(2)}) copy-start(f32[2,512,768]{2,1,0:T(8,128)} %reduce-scatter.11.cloned.1.call-done) | copy-start | bytes 9437188
  (55 other events, 240.8 us)
Sparse Core Ops, SparseCore 0:
  17.0 47.6 all-gather.4
  164.4 77.0 reduce-scatter.4
  250.6 44.9 all-gather.6
  297.1 44.9 all-gather.8
  370.6 77.0 reduce-scatter.8
  457.2 44.9 all-gather.10
  504.4 77.0 reduce-scatter.6
  645.9 76.9 reduce-scatter.10
  728.6 259.7 all-reduce.6
where the time goes:
time: 1010 us
  waiting for transfers between devices  492 us (49%)
  matrix products  196 us (19%)
  local copies, waits for them, and re-layouts  113 us (11%)
  blocking collectives  99.8 us (10%)
  other arithmetic  88.1 us (9%)
  between operations  16.4 us (2%)
    psum x1, waiting for transfers between devices, body(): lax.psum((attend_grad, query_shift_grad, value_shift_grad, out_mat_grad,...  187 us
    reduce_scatter x1, waiting for transfers between devices, body(): lax.psum_scatter(grad_hidden, 'tensor', scatter_dimension=1, tiled=True)  76.8 us
    reduce_scatter x1, waiting for transfers between devices, body(): lax.psum_scatter(partial_attn, 'tensor', scatter_dimension=1, tiled=True)  76.5 us
    psum x1, blocking collectives, body(): lax.psum((attend_grad, query_shift_grad, value_shift_grad, out_mat_grad,...  60.8 us
    all_gather x1, waiting for transfers between devices, body(): lax.all_gather(normed_two.astype(jnp.bfloat16).reshape(row_shape), 'tenso...  44.4 us
    dot_general x4, matrix products, back_product(): lax.dot_general(left, right, (((1,), (1,)), ((), ())), preferred_element_...  41 us
    psum x1, blocking collectives, body(): lax.psum((gain_one_grad, shift_one_grad, out_shift_grad, gain_two_grad, s...  39 us
    all_gather x1, waiting for transfers between devices, body(): lax.all_gather(normed_one.astype(jnp.bfloat16).reshape(row_shape), 'tenso...  38.4 us
  transfers between devices with their start and end apart: 9, of which 7 were waited for; matrix products, arithmetic and copies ran while one was open for 22% of the time, Pallas kernels for 0%

commit v1 on v0

v1 whole, which is shorter than its diff:
```python
import functools

import jax
import jax.numpy as jnp
from jax import lax
from jax.experimental import pallas as pl
from jax.experimental.pallas import tpu as pltpu
from jax.sharding import PartitionSpec as P

HD = 64
PAIR = 2 * HD
epsilon = 1e-05
masked_fill = -1e30
VMEM_LIMIT = 56 * 1024 * 1024
f32 = jnp.float32
bf16 = jnp.bfloat16


def dot_nn(left, right):
    return lax.dot_general(left, right, (((1,), (0,)), ((), ())), preferred_element_type=f32)


def dot_nt(left, right):
    return lax.dot_general(left, right, (((1,), (1,)), ((), ())), preferred_element_type=f32)


def dot_tn(left, right):
    return lax.dot_general(left, right, (((0,), (0,)), ((), ())), preferred_element_type=f32)


def select_layer(stack, layer_index):
    return lax.dynamic_index_in_dim(stack, layer_index[0], 0, keepdims=False)


def whole(shape):
    return pl.BlockSpec(shape, lambda *index: (0,) * len(shape))


def params(steps=1):
    return pltpu.CompilerParams(
        dimension_semantics=("arbitrary",) * steps, vmem_limit_bytes=VMEM_LIMIT
    )


def project_kernel(length_ref, x_ref, gain_ref, shift_ref, weight_ref, bias_ref, h_ref, qkv_ref):
    rows = x_ref.shape[0]
    x = x_ref[...].astype(f32)
    center = jnp.mean(x, axis=-1, keepdims=True)
    x = x - center
    spread = jnp.mean(x * x, axis=-1, keepdims=True)
    h = x * lax.rsqrt(spread + epsilon) * gain_ref[...] + shift_ref[...]
    position = pl.program_id(0) * rows + lax.broadcasted_iota(jnp.int32, (rows, 1), 0)
    h = jnp.where(position < length_ref[0], h, 0.0).astype(bf16)
    h_ref[...] = h
    qkv_ref[...] = (dot_nn(h, weight_ref[...]) + bias_ref[...]).astype(bf16)


def project(length, x, gain, shift, weight, bias):
    seq_len, width = x.shape
    columns = weight.shape[1]
    rows = min(256, seq_len)
    return pl.pallas_call(
        project_kernel,
        grid=(seq_len // rows,),
        in_specs=[
            pl.BlockSpec(memory_space=pltpu.SMEM),
            pl.BlockSpec((rows, width), lambda i: (i, 0)),
            whole((1, width)),
            whole((1, width)),
            whole((width, columns)),
            whole((1, columns)),
        ],
        out_specs=[
            pl.BlockSpec((rows, width), lambda i: (i, 0)),
            pl.BlockSpec((rows, columns), lambda i: (i, 0)),
        ],
        out_shape=[
            jax.ShapeDtypeStruct((seq_len, width), bf16),
            jax.ShapeDtypeStruct((seq_len, columns), bf16),
        ],
        compiler_params=params(),
        name="project",
    )(length, x, gain, shift, weight, bias)


def lane_index(rows):
    return lax.broadcasted_iota(jnp.int32, (rows, PAIR), 1)


def causal_block(block):
    row = lax.broadcasted_iota(jnp.int32, (block, block), 0)
    column = lax.broadcasted_iota(jnp.int32, (block, block), 1)
    return row, column


def attend_kernel(length_ref, q_ref, k_ref, v_ref, o_ref, lse_ref, *, block):
    seq_len = q_ref.shape[0]
    lane = lane_index(seq_len)
    position = lax.broadcasted_iota(jnp.int32, (seq_len, PAIR), 0)
    key_bias = jnp.where(position < length_ref[0], 0.0, masked_fill)
    row, column = causal_block(block)
    keep = column <= row
    q = q_ref[...].astype(f32) * (HD**-0.5)
    k = k_ref[...].astype(f32)
    values = v_ref[...]
    low = lane < HD
    outs = []
    stats = []
    for head in range(2):
        mine = low if head == 0 else jnp.logical_not(low)
        spare = HD if head == 0 else 0
        q_aug = jnp.where(mine, q, jnp.where(lane == spare, 1.0, 0.0)).astype(bf16)
        k_aug = jnp.where(mine, k, jnp.where(lane == spare, key_bias, 0.0)).astype(bf16)
        v_own = jnp.where(mine, values, jnp.zeros_like(values))
        pieces = []
        notes = []
        for index in range(seq_len // block):
            start, end = index * block, (index + 1) * block
            scores = dot_nt(q_aug[start:end], k_aug[:end])
            last = jnp.where(keep, scores[:, start:end], masked_fill)
            if index:
                scores = jnp.concatenate([scores[:, :start], last], axis=1)
            else:
                scores = last
            top = jnp.max(scores, axis=-1, keepdims=True)
            weights = jnp.exp(scores - top)
            total = jnp.sum(weights, axis=-1, keepdims=True)
            mixed = dot_nn(weights.astype(bf16), v_own[:end])
            pieces.append(mixed * (1.0 / total))
            notes.append(jnp.broadcast_to(top + jnp.log(total), (block, PAIR)))
        outs.append(jnp.concatenate(pieces, axis=0))
        stats.append(jnp.concatenate(notes, axis=0))
    o_ref[...] = (outs[0] + outs[1]).astype(bf16)
    lse_ref[...] = jnp.where(low, stats[1], stats[0])


def attend(length, qkv):
    seq_len = qkv.shape[0]
    width = qkv.shape[1] // 3
    pairs = width // PAIR
    block = min(256, seq_len)

    def columns(part):
        return pl.BlockSpec((seq_len, PAIR), lambda i: (0, part * pairs + i))

    return pl.pallas_call(
        functools.partial(attend_kernel, block=block),
        grid=(pairs,),
        in_specs=[pl.BlockSpec(memory_space=pltpu.SMEM), columns(0), columns(1), columns(2)],
        out_specs=[columns(0), columns(0)],
        out_shape=[
            jax.ShapeDtypeStruct((seq_len, width), bf16),
            jax.ShapeDtypeStruct((seq_len, width), f32),
        ],
        compiler_params=params(),
        name="attend",
    )(length, qkv, qkv, qkv)


def three_parts(values):
    first = values.astype(bf16).astype(f32)
    rest = values - first
    second = rest.astype(bf16).astype(f32)
    return first, second, rest - second


def attend_back_kernel(
    length_ref, q_ref, k_ref, v_ref, o_ref, lse_ref, go_ref, gq_ref, gk_ref, gv_ref, acc_ref, *, block
):
    seq_len = q_ref.shape[0]
    scale = HD**-0.5
    lane = lane_index(seq_len)
    position = lax.broadcasted_iota(jnp.int32, (seq_len, PAIR), 0)
    inside = position < length_ref[0]
    key_bias = jnp.where(inside, 0.0, masked_fill)
    row, column = causal_block(block)
    keep = row <= column
    q = q_ref[...]
    k = k_ref[...]
    v = v_ref[...]
    go = go_ref[...]
    q_wide = q.astype(f32) * scale
    k_wide = k.astype(f32)
    v_wide = v.astype(f32)
    go_wide = go.astype(f32)
    both = go_wide * o_ref[...].astype(f32)
    lse_parts = three_parts(-lse_ref[...])
    low = lane < HD
    zero = jnp.zeros_like(q)
    acc_ref[...] = jnp.zeros_like(acc_ref)
    count = seq_len // block
    grads_k = [None] * count
    grads_v = [None] * count
    for head in range(2):
        mine = low if head == 0 else jnp.logical_not(low)
        spare = HD if head == 0 else 0
        delta = jnp.sum(jnp.where(mine, both, 0.0), axis=-1, keepdims=True)
        delta_parts = three_parts(-jnp.broadcast_to(delta, (seq_len, PAIR)))

        def extras(parts):
            return jnp.where(
                lane == spare + 1,
                parts[0],
                jnp.where(lane == spare + 2, parts[1], jnp.where(lane == spare + 3, parts[2], 0.0)),
            )

        ones = jnp.where((lane > spare) & (lane < spare + 4), 1.0, 0.0)
        q_aug = jnp.where(mine, q_wide, jnp.where(lane == spare, 1.0, extras(lse_parts))).astype(bf16)
        k_aug = jnp.where(mine, k_wide, jnp.where(lane == spare, key_bias, ones)).astype(bf16)
        v_aug = jnp.where(mine, v_wide, ones).astype(bf16)
        go_aug = jnp.where(mine, go_wide, extras(delta_parts)).astype(bf16)
        q_own = jnp.where(mine, q, zero)
        k_own = jnp.where(mine, k, zero)
        go_own = jnp.where(mine, go, zero)
        for index in range(count):
            start, end = index * block, (index + 1) * block
            scores = dot_nt(k_aug[start:end], q_aug[start:])
            first = jnp.where(keep, scores[:, :block], masked_fill)
            if index + 1 < count:
                scores = jnp.concatenate([first, scores[:, block:]], axis=1)
            else:
                scores = first
            shares = jnp.exp(scores)
            moved = dot_nt(v_aug[start:end], go_aug[start:])
            grad_scores = (shares * moved).astype(bf16)
            grad_v = dot_nn(shares.astype(bf16), go_own[start:])
            grad_k = dot_nn(grad_scores, q_own[start:])
            grads_v[index] = grad_v if head == 0 else grads_v[index] + grad_v
            grads_k[index] = grad_k if head == 0 else grads_k[index] + grad_k
            acc_ref[start:, :] += dot_tn(grad_scores, k_own[start:end])
    gq_ref[...] = (acc_ref[...] * scale).astype(bf16)
    gk_ref[...] = (jnp.concatenate(grads_k, axis=0) * scale).astype(bf16)
    gv_ref[...] = jnp.where(inside, jnp.concatenate(grads_v, axis=0), 0.0).astype(bf16)


def attend_back(length, qkv, o, lse, go):
    seq_len = qkv.shape[0]
    width = qkv.shape[1] // 3
    pairs = width // PAIR
    block = min(256, seq_len)

    def columns(part):
        return pl.BlockSpec((seq_len, PAIR), lambda i: (0, part * pairs + i))

    one = jax.ShapeDtypeStruct((seq_len, width), bf16)
    return pl.pallas_call(
        functools.partial(attend_back_kernel, block=block),
        grid=(pairs,),
        in_specs=[pl.BlockSpec(memory_space=pltpu.SMEM)]
        + [columns(0), columns(1), columns(2)]
        + [columns(0)] * 3,
        out_specs=[columns(0)] * 3,
        out_shape=[one, one, one],
        scratch_shapes=[pltpu.VMEM((seq_len, PAIR), f32)],
        compiler_params=params(),
        name="attend_back",
    )(length, qkv, qkv, qkv, o, lse, go)


def feed_kernel(
    h_ref, gf_ref, e_ref, b_ref, s_ref, *rest, chunk, carried
):
    if carried:
        f_in, gh_in, f_ref, gh_ref, de_ref, ds_ref, db_ref, act_ref, gu_ref = rest
    else:
        f_ref, gh_ref, de_ref, ds_ref, db_ref, act_ref, gu_ref = rest
    seq_len = h_ref.shape[0]
    tile = e_ref.shape[1]
    root = 0.7978845608
    cube = 0.044715

    @pl.when(pl.program_id(0) == 0)
    def _():
        if carried:
            f_ref[...] = f_in[...]
            gh_ref[...] = gh_in[...]
        else:
            f_ref[...] = jnp.zeros_like(f_ref)
            gh_ref[...] = jnp.zeros_like(gh_ref)

    e = e_ref[...]
    s = s_ref[...]
    bias = b_ref[...]
    total = jnp.zeros((1, tile), f32)
    for index in range(seq_len // chunk):
        rows = pl.ds(index * chunk, chunk)
        u = dot_nn(h_ref[rows, :], e) + bias
        ga = dot_nt(gf_ref[rows, :], s)
        square = u * u
        bent = jnp.tanh(u * (root + (root * cube) * square))
        half = 0.5 + 0.5 * bent
        act = (u * half).astype(bf16)
        slope = half + (0.5 * u) * (1.0 - bent * bent) * (root + (3.0 * root * cube) * square)
        gu_wide = (slope * ga).astype(bf16)
        act_ref[rows, :] = act
        gu_ref[rows, :] = gu_wide
        total += jnp.sum(gu_wide.astype(f32), axis=0, keepdims=True)
        f_ref[rows, :] += dot_nn(act, s)
        gh_ref[rows, :] += dot_nt(gu_wide, e)
    db_ref[...] = total
    ds_ref[...] = dot_tn(act_ref[...], gf_ref[...]).astype(bf16)
    de_ref[...] = dot_tn(h_ref[...], gu_ref[...]).astype(bf16)


def feed(h, gf, expand, bias, shrink, carry=None):
    seq_len, width = h.shape
    hidden = expand.shape[1]
    tile = min(512, hidden)
    chunk = min(256, seq_len)
    rows = whole((seq_len, width))
    row_shape = jax.ShapeDtypeStruct((seq_len, width), f32)
    carried = carry is not None
    return pl.pallas_call(
        functools.partial(feed_kernel, chunk=chunk, carried=carried),
        grid=(hidden // tile,),
        in_specs=[
            rows,
            rows,
            pl.BlockSpec((width, tile), lambda i: (0, i)),
            pl.BlockSpec((1, tile), lambda i: (0, i)),
            pl.BlockSpec((tile, width), lambda i: (i, 0)),
        ]
        + ([rows, rows] if carried else []),
        out_specs=[
            rows,
            rows,
            pl.BlockSpec((width, tile), lambda i: (0, i)),
            pl.BlockSpec((tile, width), lambda i: (i, 0)),
            pl.BlockSpec((1, tile), lambda i: (0, i)),
        ],
        out_shape=[
            row_shape,
            row_shape,
            jax.ShapeDtypeStruct((width, hidden), bf16),
            jax.ShapeDtypeStruct((hidden, width), bf16),
            jax.ShapeDtypeStruct((1, hidden), f32),
        ],
        scratch_shapes=[pltpu.VMEM((seq_len, tile), bf16), pltpu.VMEM((seq_len, tile), bf16)],
        compiler_params=params(),
        name="feed",
    )(h, gf, expand, bias, shrink, *(carry if carried else ()))


def norm_parts(values):
    center = jnp.mean(values, axis=-1, keepdims=True)
    centered = values - center
    spread = jnp.mean(centered * centered, axis=-1, keepdims=True)
    inverse = lax.rsqrt(spread + epsilon)
    return centered * inverse, inverse


def norm_back(unit, inverse, gain, grad):
    scaled = grad * gain
    return inverse * (
        scaled
        - jnp.mean(scaled, axis=-1, keepdims=True)
        - unit * jnp.mean(scaled * unit, axis=-1, keepdims=True)
    )


def body(
    tokens,
    lengths,
    layer_index,
    norm_one_gain,
    norm_one_bias,
    attend_weight,
    query_bias,
    value_bias,
    output_weight,
    output_bias,
    norm_two_gain,
    norm_two_bias,
    expand_weight,
    expand_bias,
    shrink_weight,
    shrink_bias,
    cotangent,
):
    seq_dev, half, width = tokens.shape
    seq_len = 2 * half
    dp = lax.axis_size("dp")
    here = lax.axis_index("tensor")
    there = 1 - here
    place = lax.axis_index("dp")
    swap = [(0, 1), (1, 0)]

    def exchange(values):
        return lax.ppermute(values, "tensor", swap)

    def pick(values, index):
        return lax.dynamic_index_in_dim(values, index, 0, keepdims=False)

    def joined(mine, other):
        out = jnp.zeros((seq_len,) + mine.shape[1:], mine.dtype)
        out = lax.dynamic_update_slice_in_dim(out, mine, here * half, 0)
        return lax.dynamic_update_slice_in_dim(out, other, there * half, 0)

    def rows_of(values, index):
        return lax.dynamic_slice_in_dim(values, index * half, half, 0)

    def layer(stack):
        return select_layer(stack, layer_index)

    x_far = joined(pick(tokens, there), exchange(pick(tokens, here)))
    x_own = joined(pick(tokens, here), exchange(pick(tokens, there)))
    len_far = lax.dynamic_slice_in_dim(lengths, there, 1, 0)
    len_own = lax.dynamic_slice_in_dim(lengths, here, 1, 0)
    cot_own = joined(pick(cotangent, here), exchange(pick(cotangent, there)))

    gain_one = layer(norm_one_gain).astype(f32)[None]
    shift_one = layer(norm_one_bias).astype(f32)[None]
    gain_two = layer(norm_two_gain).astype(f32)[None]
    shift_two = layer(norm_two_bias).astype(f32)[None]
    attend_flat = layer(attend_weight).reshape(width, -1)
    local = attend_flat.shape[1] // 3
    qkv_bias = jnp.concatenate(
        [layer(query_bias).astype(f32), jnp.zeros((local,), f32), layer(value_bias).astype(f32)]
    )[None]
    out_mat = layer(output_weight)
    out_shift = layer(output_bias).astype(f32)[None]
    expand_mat = layer(expand_weight)
    expand_shift = layer(expand_bias).astype(f32)[None]
    shrink_mat = layer(shrink_weight)
    shrink_shift = layer(shrink_bias).astype(f32)[None]

    def fetch(matrix):
        share = matrix.shape[0] // dp
        piece = lax.dynamic_slice_in_dim(matrix, place * share, share, 0)
        return lax.all_gather(exchange(piece), "dp", axis=0, tiled=True)

    out_far = fetch(out_mat)
    shrink_far = fetch(shrink_mat)
    expand_far = fetch(expand_mat)
    expand_shift_far = exchange(layer(expand_bias))[None].astype(f32)

    h_far, qkv_far = project(len_far, x_far, gain_one, shift_one, attend_flat, qkv_bias)
    o_far, lse_far = attend(len_far, qkv_far)
    o_got = exchange(o_far)
    h_own, qkv_own = project(len_own, x_own, gain_one, shift_one, attend_flat, qkv_bias)
    o_own, lse_own = attend(len_own, qkv_own)

    valid = (lax.broadcasted_iota(jnp.int32, (seq_len, 1), 0) < len_own[0]).astype(f32)
    attn = dot_nn(o_own, out_mat) + dot_nn(o_got, out_far) + out_shift
    resid = x_own.astype(f32) + valid * attn
    unit_two, inverse_two = norm_parts(resid)
    h_two = (valid * (unit_two * gain_two + shift_two)).astype(bf16)
    cot = cot_own.astype(f32)
    gf_wide = valid * cot
    gf = gf_wide.astype(bf16)

    f_part, gh_part, de_own, ds_own, db_own = feed(h_two, gf, expand_mat, expand_shift, shrink_mat)
    f_sum, gh_two, de_far, ds_far, db_far = feed(
        h_two, gf, expand_far, expand_shift_far, shrink_far, (f_part, gh_part)
    )
    mlp = f_sum + shrink_shift
    result = resid + valid * mlp
    result_got = exchange(rows_of(result, there).astype(bf16))

    grad_norm = valid * gh_two
    grad_resid = cot + norm_back(unit_two, inverse_two, gain_two, grad_norm)
    gain_two_grad = jnp.sum(grad_norm * unit_two, axis=0)
    shift_two_grad = jnp.sum(grad_norm, axis=0)
    grad_attn = valid * grad_resid
    ga = grad_attn.astype(bf16)
    go_send = dot_nt(ga, out_far).astype(bf16)
    go_far = exchange(go_send)
    go_own = dot_nt(ga, out_mat).astype(bf16)
    do_own = dot_tn(o_own, ga).astype(bf16)
    do_far = dot_tn(o_got, ga).astype(bf16)

    gq_own, gk_own, gv_own = attend_back(len_own, qkv_own, o_own, lse_own, go_own)

    def back_rows(gq, gk, gv, x, length):
        stacked = jnp.concatenate([gq, gk, gv], axis=1)
        inside = (lax.broadcasted_iota(jnp.int32, (seq_len, 1), 0) < length[0]).astype(f32)
        partial = inside * dot_nt(stacked, attend_flat)
        unit, inverse = norm_parts(x.astype(f32))
        return (
            stacked,
            norm_back(unit, inverse, gain_one, partial),
            jnp.sum(partial * unit, axis=0),
            jnp.sum(partial, axis=0),
        )

    stack_own, back_own, gain_own, shift_own = back_rows(gq_own, gk_own, gv_own, x_own, len_own)
    back_own = grad_resid + back_own
    in_far_got = exchange(rows_of(back_own, there).astype(bf16))

    gq_far, gk_far, gv_far = attend_back(len_far, qkv_far, o_far, lse_far, go_far)
    stack_far, back_far, gain_far, shift_far = back_rows(gq_far, gk_far, gv_far, x_far, len_far)
    in_own_got = exchange(rows_of(back_far, there).astype(bf16))
    da = (dot_tn(h_own, stack_own) + dot_tn(h_far, stack_far)).astype(bf16)

    input_own = rows_of(back_own, here) + in_own_got.astype(f32)
    input_far = rows_of(back_far, here) + in_far_got.astype(f32)

    def by_sequence(own, far):
        out = jnp.zeros((2,) + own.shape, own.dtype)
        out = lax.dynamic_update_index_in_dim(out, own, here, 0)
        return lax.dynamic_update_index_in_dim(out, far, there, 0)

    block_output = by_sequence(rows_of(result, here), result_got.astype(f32))
    input_grad = by_sequence(input_own, input_far)

    def by_half(own, far):
        return by_sequence(own, far).reshape((2 * own.shape[0],) + own.shape[1:])

    def total(own, far):
        share = lax.psum_scatter(
            by_half(own, far), ("tensor", "dp"), scatter_dimension=0, tiled=True
        )
        return lax.all_gather(share, "dp", axis=0, tiled=True).astype(f32)

    shrink_grad = total(ds_own, ds_far)
    expand_grad = total(de_own, de_far)
    out_grad = total(do_own, do_far)
    attend_grad = lax.psum(da, "dp").astype(f32).reshape(width, 3, local)
    expand_shift_grad = by_sequence(db_own[0], db_far[0])
    qv_bias = jnp.stack(
        [
            jnp.sum(gq_own.astype(f32), axis=0) + jnp.sum(gq_far.astype(f32), axis=0),
            jnp.sum(gv_own.astype(f32), axis=0) + jnp.sum(gv_far.astype(f32), axis=0),
        ]
    )
    bias_grads = by_sequence(qv_bias, jnp.zeros_like(qv_bias))
    counters = jnp.stack(
        [
            jnp.sum(valid * result * result),
            jnp.sum(valid * attn * attn),
            jnp.sum(valid * mlp * mlp),
            jnp.sum(valid),
        ]
    )
    small = lax.psum(
        (
            gain_own + gain_far,
            shift_own + shift_far,
            jnp.sum(grad_attn, axis=0),
            gain_two_grad,
            shift_two_grad,
            jnp.sum(gf_wide, axis=0),
            counters,
            expand_shift_grad,
            bias_grads,
        ),
        ("dp", "tensor"),
    )
    rms_values = jnp.sqrt(small[6][:3] / (small[6][3] * width))
    biases = pick(small[8], here)
    return (
        block_output,
        input_grad,
        small[0],
        small[1],
        attend_grad,
        biases[0],
        biases[1],
        out_grad,
        small[2],
        small[3],
        small[4],
        expand_grad,
        pick(small[7], here),
        shrink_grad,
        small[5],
        rms_values,
    )


def solution(mesh):
    in_specs = (
        P("dp", "tensor", None),
        P("dp"),
        P(),
        P(),
        P(),
        P(None, None, None, "tensor"),
        P(None, "tensor"),
        P(None, "tensor"),
        P(None, "tensor", None),
        P(),
        P(),
        P(),
        P(None, None, "tensor"),
        P(None, "tensor"),
        P(None, "tensor", None),
        P(),
        P("dp", "tensor", None),
    )
    out_specs = (
        P("dp", "tensor", None),
        P("dp", "tensor", None),
        P(),
        P(),
        P(None, None, "tensor"),
        P("tensor"),
        P("tensor"),
        P("tensor", None),
        P(),
        P(),
        P(),
        P(None, "tensor"),
        P("tensor"),
        P("tensor", None),
        P(),
        P(),
    )
    return jax.shard_map(body, mesh=mesh, in_specs=in_specs, out_specs=out_specs, check_vma=False)
```

time: 1010 us -> 754 us (0.75)
  matrix products: 196 us -> 26.7 us
  waiting for transfers between devices: 492 us -> 334 us
  Pallas kernels: 0 us -> 117 us
  local copies, waits for them, and re-layouts: 113 us -> 72.2 us
  other arithmetic: 88.1 us -> 56.9 us
  starting transfers between devices: 0.95 us -> 17.5 us
    dot_general x24 -> x10, matrix products: 196 us -> 26.7 us  [the longest x4 13.4 us: dot_nt(): lax.dot_general(left, right, (((1,), (1,)), ((), ())), preferred_element_...]
    psum x1, waiting for transfers between devices: 187 us -> 69.5 us  [body(): attend_grad = lax.psum(da, 'dp').astype(f32).reshape(width, 3, local)]
    pallas_call x0 -> x8, Pallas kernels: none -> 117 us  [the longest x2 42.8 us: feed(): pl.pallas_call(functools.partial(feed_kernel, chunk=chunk, carried=carrie...]
    all_gather x4, waiting for transfers between devices: 151 us -> 78.8 us  [the longest x2 78.8 us: total(): return lax.all_gather(share, 'dp', axis=0, tiled=True).astype(f32)]
    all_gather x0 -> x2, blocking collectives: none -> 48.1 us  [the longest x1 25.3 us: fetch(): return lax.all_gather(exchange(piece), 'dp', axis=0, tiled=True)]
    ppermute x0 -> x12, waiting for transfers between devices: none -> 45.2 us  [exchange(): return lax.ppermute(values, 'tensor', swap)]
    psum x2 -> x1, blocking collectives: 99.8 us -> 60.1 us  [body(): lax.psum((gain_own + gain_far, shift_own + shift_far, jnp.sum(grad_attn,...]
    dynamic_update_slice x0 -> x14, local copies, waits for them, and re-layouts: none -> 21.5 us  [the longest x3 6.25 us: joined(): return lax.dynamic_update_slice_in_dim(out, other, there * half, 0)]
  transfers between devices with their start and end apart: 9 -> 20, of which waited for: 7 -> 8; matrix products, arithmetic and copies ran while one was open for 22% -> 19% of each run, Pallas kernels for 0% -> 13%
where the time goes in v1:
time: 754 us; the launch traced here: 749 us
  waiting for transfers between devices  334 us (44%)
  Pallas kernels  117 us (16%)
  blocking collectives  108 us (14%)
  local copies, waits for them, and re-layouts  72.2 us (10%)
  other arithmetic  56.9 us (8%)
  matrix products  26.7 us (4%)
  starting transfers between devices  17.5 us (2%)
  between operations  16.6 us (2%)
    reduce_scatter x3, waiting for transfers between devices, total(): lax.psum_scatter(by_half(own, far), ('tensor', 'dp'), scatter_dimension=0...  140 us
    all_gather x2, waiting for transfers between devices, total(): return lax.all_gather(share, 'dp', axis=0, tiled=True).astype(f32)  78.8 us
    psum x1, waiting for transfers between devices, body(): attend_grad = lax.psum(da, 'dp').astype(f32).reshape(width, 3, local)  69.5 us
    psum x1, blocking collectives, body(): lax.psum((gain_own + gain_far, shift_own + shift_far, jnp.sum(grad_attn,...  60.1 us
    ppermute x12, waiting for transfers between devices, exchange(): return lax.ppermute(values, 'tensor', swap)  45.2 us
    pallas_call x2, Pallas kernels, feed(): pl.pallas_call(functools.partial(feed_kernel, chunk=chunk, carried=carrie...  42.8 us
    pallas_call x2, Pallas kernels, attend_back(): pl.pallas_call(functools.partial(attend_back_kernel, block=block), grid=(...  34.2 us
    pallas_call x2, Pallas kernels, attend(): pl.pallas_call(functools.partial(attend_kernel, block=block), grid=(pairs...  25.8 us
  transfers between devices with their start and end apart: 20, of which 8 were waited for; matrix products, arithmetic and copies ran while one was open for 19% of the time, Pallas kernels for 13%

profile of v1, /device:TPU:0, one launch (start us, length us, event | category | flops | bytes accessed | tf_op | source)
XLA Modules:
  0.0 749.0 jit_solution(69221651862509095)
XLA Ops:
  35.7 41.3 %collective-permute-done.7 = bf16[96,768]{1,0:T(8,128)(2,1)S(1)} collective-permute-done((bf16[96,768]{1,0:T(8,128)(2,1)S(1)}, bf16[96,768]{1,0:T(8,128)(2,1)S(1)}, u32[]{:S(2)}, u32[]{:S(2)}) %collective-permute-start.7) | collective-permute-done | bytes 147488 | tf_op jit(solution)/shard_map/ppermute | solution.py:389
  98.3 25.3 %all_gather.18 = bf16[384,768]{1,0:T(8,128)(2,1)S(1)} all-gather(bf16[24,768]{1,0:T(8,128)(2,1)S(1)} %collective-permute-done.3), channel_id=1, replica_groups=mesh['dp'=16,'tensor'=2] {'dp'}, dimensions={0}, use_global_device_ids=true | all-gather | bytes 626688 | tf_op jit(solution)/shard_map/all_gather | solution.py:430
  125.6 7.1 project.3
  132.8 12.9 %attend.3 = (bf16[1024,384]{1,0:T(8,128)(2,1)}, f32[1024,384]{1,0:T(8,128)}) custom-call(s32[1]{0:T(128)} %get-tuple-element.155.length_ref, bf16[1024,1152]{1,0:T(8,128)(2,1)} %get-tuple-element.42.q_ref.k_ref.v_ref, bf16[1024,1152]{1,0:T(8,128)(2,1)} %get-tuple-element.42.q_ref.k_ref.v_ref, bf16[1024,1152]{1,0:T(8,128)(2,1)} %get-tuple-element.42.q_ref.k_ref.v_ref), custom_call_target="tpu_custom_call" | custom-call | tf_op jit(solution)/shard_map/attend/pallas_call | solution.py:146
  150.2 7.2 project.2
  157.4 12.9 %attend.2 = (bf16[1024,384]{1,0:T(8,128)(2,1)}, f32[1024,384]{1,0:T(8,128)}) custom-call(s32[1]{0:T(128)} %get-tuple-element.156.length_ref, bf16[1024,1152]{1,0:T(8,128)(2,1)} %get-tuple-element.40.q_ref.k_ref.v_ref, bf16[1024,1152]{1,0:T(8,128)(2,1)} %get-tuple-element.40.q_ref.k_ref.v_ref, bf16[1024,1152]{1,0:T(8,128)(2,1)} %get-tuple-element.40.q_ref.k_ref.v_ref), custom_call_target="tpu_custom_call" | custom-call | tf_op jit(solution)/shard_map/attend/pallas_call | solution.py:146
  174.1 5.0 fusion.62
  181.8 20.6 %feed.2 = (f32[1024,768]{1,0:T(8,128)}, f32[1024,768]{1,0:T(8,128)}, bf16[768,1536]{1,0:T(8,128)(2,1)}, bf16[1536,768]{1,0:T(8,128)(2,1)}, f32[1,1536]{1,0:T(1,128)}) custom-call(bf16[1024,768]{1,0:T(8,128)(2,1)} %multiply_convert_fusion.h_ref, bf16[1024,768]{1,0:T(8,128)(2,1)} %get-tuple-element.142.gf_ref, ...), custom_call_target="tpu_custom_call" | custom-call | tf_op jit(solution)/shard_map/feed/pallas_call | solution.py:313
  206.6 22.2 %feed.3 = (f32[1024,768]{1,0:T(8,128)}, f32[1024,768]{1,0:T(8,128)}, bf16[768,1536]{1,0:T(8,128)(2,1)}, bf16[1536,768]{1,0:T(8,128)(2,1)}, f32[1,1536]{1,0:T(1,128)}) custom-call(bf16[1024,768]{1,0:T(8,128)(2,1)} %multiply_convert_fusion.h_ref, bf16[1024,768]{1,0:T(8,128)(2,1)} %get-tuple-element.142.gf_ref, ...), custom_call_target="tpu_custom_call" | custom-call | tf_op jit(solution)/shard_map/feed/pallas_call | solution.py:313
  239.4 4.8 multiply_reduce_fusion
  254.6 17.1 %attend_back.2 = (bf16[1024,384]{1,0:T(8,128)(2,1)}, bf16[1024,384]{1,0:T(8,128)(2,1)}, bf16[1024,384]{1,0:T(8,128)(2,1)}) custom-call(s32[1]{0:T(128)} %get-tuple-element.156.length_ref, bf16[1024,1152]{1,0:T(8,128)(2,1)} %get-tuple-element.40.q_ref.k_ref.v_ref, bf16[1024,1152]{1,0:T(8,128)(2,1)} %get-tuple-element.40.q_ref.k_ref.v_ref, ...), custom_call_target="tpu_custom_call" | custom-call | tf_op jit(solution)/shard_map/attend_back/pallas_call | solution.py:246
  274.5 17.1 %attend_back.3 = (bf16[1024,384]{1,0:T(8,128)(2,1)}, bf16[1024,384]{1,0:T(8,128)(2,1)}, bf16[1024,384]{1,0:T(8,128)(2,1)}) custom-call(s32[1]{0:T(128)} %get-tuple-element.155.length_ref, bf16[1024,1152]{1,0:T(8,128)(2,1)} %get-tuple-element.42.q_ref.k_ref.v_ref, bf16[1024,1152]{1,0:T(8,128)(2,1)} %get-tuple-element.42.q_ref.k_ref.v_ref, ...), custom_call_target="tpu_custom_call" | custom-call | tf_op jit(solution)/shard_map/attend_back/pallas_call | solution.py:246
  301.5 35.0 %reduce-scatter.6.cloned.1.call-done = bf16[48,1536]{1,0:T(8,128)(2,1)} async-done(((bf16[1536,1536]{1,0:T(8,128)(2,1)}), bf16[48,1536]{1,0:T(8,128)(2,1)}) %reduce-scatter.6.cloned.1.call-update) | async-done | bytes 147472 | tf_op jit(solution)/shard_map/reduce_scatter | solution.py:510
  345.4 5.7 fusion.64
  354.9 94.6 %reduce-scatter.8.cloned.1.call-done = bf16[96,768]{1,0:T(8,128)(2,1)} async-done(((bf16[3072,768]{1,0:T(8,128)(2,1)}), bf16[96,768]{1,0:T(8,128)(2,1)}) %reduce-scatter.8.cloned.1.call-update) | async-done | bytes 147472 | tf_op jit(solution)/shard_map/reduce_scatter | solution.py:510
  449.6 11.3 %fusion.22 = (f32[768]{0:T(1024)S(1)}, f32[1024]{0:T(1024)S(1)}, f32[1024]{0:T(1024)S(1)}, f32[768]{0:T(1024)S(1)}, f32[768]{0:T(1024)S(1)}, /*index=5*/f32[1024...) fusion(bf16[1024,768]{1,0:T(8,128)(2,1)} %constant_dynamic-upda, ...), kind=kLoop, calls=%fused_computation.34 | loop fusion | flops 29875712 | bytes 26804236 | tf_op jit(solution)/shard_map/reduce_sum | solution.py:482
  474.6 60.1 %all-reduce = (f32[768]{0:T(1024)}, f32[768]{0:T(1024)}, f32[2,2,384]{2,1,0:T(2,128)S(1)}, f32[768]{0:T(1024)}, f32[768]{0:T(1024)}, /*index=5*/f32[768]{0:T(102...) all-reduce(f32[768]{0:T(1024)S(1)} %add.270, ...), channel_id=1, replica_groups=mesh['dp'=16,'tensor'=2] {'dp','tensor'}, use_global_device_ids=true, to_apply=%region_14.15 | all-reduce | flops 9220 | bytes 73760 | tf_op jit(solution)/shard_map/psum | solution.py:535
  539.8 10.6 %reduce-scatter.4.cloned.1.call-done = bf16[24,768]{1,0:T(8,128)(2,1)} async-done(((bf16[768,768]{1,0:T(8,128)(2,1)}), bf16[24,768]{1,0:T(8,128)(2,1)}) %reduce-scatter.4.cloned.1.call-update) | async-done | bytes 36880 | tf_op jit(solution)/shard_map/reduce_scatter | solution.py:510
  550.4 22.8 %all_gather.21 = bf16[384,768]{1,0:T(8,128)(2,1)S(1)} all-gather(bf16[24,768]{1,0:T(8,128)(2,1)} %reduce-scatter.4.cloned.1.call-done), channel_id=1, replica_groups=mesh['dp'=16,'tensor'=2] {'dp'}, dimensions={0}, use_global_device_ids=true | all-gather | bytes 626688 | tf_op jit(solution)/shard_map/all_gather | solution.py:513
  580.7 69.5 %all-reduce.3.cloned.1.call-done = bf16[768,3,384]{0,2,1:T(8,128)(2,1)} async-done(((bf16[768,3,384]{0,2,1:T(8,128)(2,1)}), bf16[768,3,384]{0,2,1:T(8,128)(2,1)}) %all-reduce.3.cloned.1.call-update) | async-done | bytes 1769488 | tf_op jit(solution)/shard_map/psum | solution.py:518
  654.2 39.8 %all-gather.9.cloned.1.call-done = bf16[768,1536]{1,0:T(8,128)(2,1)} async-done(((bf16[48,1536]{1,0:T(8,128)(2,1)}), bf16[768,1536]{1,0:T(8,128)(2,1)}) %all-gather.9.cloned.1.call-update) | async-done | bytes 2359312 | tf_op jit(solution)/shard_map/all_gather | solution.py:513
  694.0 4.6 convert_element_type.164
  698.7 39.0 %all-gather.11.cloned.1.call-done = bf16[1536,768]{1,0:T(8,128)(2,1)} async-done(((bf16[96,768]{1,0:T(8,128)(2,1)}), bf16[1536,768]{1,0:T(8,128)(2,1)}) %all-gather.11.cloned.1.call-update) | async-done | bytes 2359312 | tf_op jit(solution)/shard_map/all_gather | solution.py:513
  737.7 4.2 convert_element_type.165
  (245 shorter events, 141.6 us)
Async XLA Ops:
  7.2 199.4 %all-gather.5.cloned.1.call-start = ((), (), s32[]{:S(2)}) async-start(), calls=%async_computation.3 | async-start | bytes 2506752 | tf_op jit(solution)/shard_map/all_gather | solution.py:430
  9.0 6.9 collective-permute-start.5
  16.6 190.0 %all-gather.7.cloned.1.call-start = ((), (), s32[]{:S(2)}) async-start(), calls=%async_computation.4 | async-start | bytes 2506752 | tf_op jit(solution)/shard_map/all_gather | solution.py:430
  20.3 125.7 %collective-permute-start = (bf16[512,768]{1,0:T(8,128)(2,1)}, bf16[512,768]{1,0:T(8,128)(2,1)}, u32[]{:S(2)}, u32[]{:S(2)}) collective-permute-start(bf16[512,768]{1,0:T(8,128)(2,1)} %get-tuple-element.136), channel_id=1, source_target_pairs={{0,1},{1,0},{2,3},{3,2},{4,5},{5,4},{6,7},{7,6},{8,9},{9,8},{10,11... | collective-permute-start | bytes 2359304 | tf_op jit(solution)/shard_map/ppermute | solution.py:389
  25.7 97.8 %collective-permute-start.1 = (bf16[512,768]{1,0:T(8,128)(2,1)}, bf16[512,768]{1,0:T(8,128)(2,1)}, u32[]{:S(2)}, u32[]{:S(2)}) collective-permute-start(bf16[512,768]{1,0:T(8,128)(2,1)} %get-tuple-element.138), channel_id=1, source_target_pairs={{0,1},{1,0},{2,3},{3,2},{4,5},{5,4},{6,7},{7,6},{8,9},{9,8},{10,11... | collective-permute-start | bytes 2359304 | tf_op jit(solution)/shard_map/ppermute | solution.py:389
  27.0 121.2 %collective-permute-start.4 = (bf16[512,768]{1,0:T(8,128)(2,1)}, bf16[512,768]{1,0:T(8,128)(2,1)}, u32[]{:S(2)}, u32[]{:S(2)}) collective-permute-start(bf16[512,768]{1,0:T(8,128)(2,1)} %dynamic-slice_bitcast_fusion.2), channel_id=1, source_target_pairs={{0,1},{1,0},{2,3},{3,2},{4,5},{5,4},{6,7},{7,6},{8,9},{9,8},{10,11... | collective-permute-start | bytes 2359304 | tf_op jit(solution)/shard_map/ppermute | solution.py:389
  28.7 69.6 %collective-permute-start.3 = (bf16[24,768]{1,0:T(8,128)(2,1)S(1)}, bf16[24,768]{1,0:T(8,128)(2,1)S(1)}, u32[]{:S(2)}, u32[]{:S(2)}) collective-permute-start(bf16[24,768]{1,0:T(8,128)(2,1)S(1)} %dynamic-slice_bitcast_fusion.7), channel_id=1, source_target_pairs={{0,1},{1,0},{2,3},{3,2},{4,5},{5,4},{6,7},{7,6},{8,9},{9,8},{10,11... | collective-permute-start | bytes 110600 | tf_op jit(solution)/shard_map/ppermute | solution.py:389
  30.1 46.9 %collective-permute-start.7 = (bf16[96,768]{1,0:T(8,128)(2,1)S(1)}, bf16[96,768]{1,0:T(8,128)(2,1)S(1)}, u32[]{:S(2)}, u32[]{:S(2)}) collective-permute-start(bf16[96,768]{1,0:T(8,128)(2,1)S(1)} %dynamic-slice_bitcast_fusion.5), channel_id=1, source_target_pairs={{0,1},{1,0},{2,3},{3,2},{4,5},{5,4},{6,7},{7,6},{8,9},{9,8},{10,11... | collective-permute-start | bytes 442376 | tf_op jit(solution)/shard_map/ppermute | solution.py:389
  35.0 46.6 %copy-start.39 = (s32[2]{0:T(128)S(1)}, s32[2]{0:T(128)}, u32[]{:S(2)}) copy-start(s32[2]{0:T(128)} %param.18) | copy-start | bytes 28
  76.9 20.7 %collective-permute-start.6 = (bf16[1536]{0:T(1024)(128)(2,1)S(1)}, bf16[1536]{0:T(1024)(128)(2,1)S(1)}, u32[]{:S(2)}, u32[]{:S(2)}) collective-permute-start(bf16[1536]{0:T(1024)(128)(2,1)S(1)} %get-tuple-element.141), channel_id=1, source_target_pairs={{0,1},{1,0},{2,3},{3,2},{4,5},{5,4},{6,7},{7,6},{8,9},{9,8},{10,11... | collective-permute-start | bytes 9224 | tf_op jit(solution)/shard_map/ppermute | solution.py:389
  78.4 258.2 %reduce-scatter.6.cloned.1.call-start = ((), (), s32[]{:S(2)}) async-start(), calls=%async_computation.7 | async-start | bytes 4866048 | tf_op jit(solution)/shard_map/reduce_scatter | solution.py:510
  145.7 28.4 %collective-permute-start.2 = (bf16[1024,384]{1,0:T(8,128)(2,1)}, bf16[1024,384]{1,0:T(8,128)(2,1)S(1)}, u32[]{:S(2)}, u32[]{:S(2)}) collective-permute-start(bf16[1024,384]{1,0:T(8,128)(2,1)} %get-tuple-element.43.o_ref), channel_id=1, source_target_pairs={{0,1},{1,0},{2,3},{3,2},{4,5},{5,4},{6,7},{7,6},{8,9},{9,8},{10,11... | collective-permute-start | bytes 2359304 | tf_op jit(solution)/shard_map/ppermute | solution.py:389
  232.1 217.5 %reduce-scatter.8.cloned.1.call-start = ((), (), s32[]{:S(2)}) async-start(), calls=%async_computation.9 | async-start | bytes 4866048 | tf_op jit(solution)/shard_map/reduce_scatter | solution.py:510
  239.3 311.1 %reduce-scatter.4.cloned.1.call-start = ((), (), s32[]{:S(2)}) async-start(), calls=%async_computation.6 | async-start | bytes 1216512 | tf_op jit(solution)/shard_map/reduce_scatter | solution.py:510
  250.1 24.3 %collective-permute-start.9 = (bf16[1024,384]{1,0:T(8,128)(2,1)}, bf16[1024,384]{1,0:T(8,128)(2,1)}, u32[]{:S(2)}, u32[]{:S(2)}) collective-permute-start(bf16[1024,384]{1,0:T(8,128)(2,1)} %convolution_convert_fusion), channel_id=1, source_target_pairs={{0,1},{1,0},{2,3},{3,2},{4,5},{5,4},{6,7},{7,6},{8,9},{9,8},{10,11... | collective-permute-start | bytes 2359304 | tf_op jit(solution)/shard_map/ppermute | solution.py:389
  273.6 376.6 %all-reduce.3.cloned.1.call-start = ((), (), s32[]{:S(2)}) async-start(), calls=%async_computation.5 | async-start | bytes 3538944 | tf_op jit(solution)/shard_map/psum | solution.py:518
  301.5 41.0 %copy-start.37 = (f32[1,1536]{1,0:T(1,128)S(1)}, f32[1,1536]{1,0:T(1,128)}, u32[]{:S(2)}) copy-start(f32[1,1536]{1,0:T(1,128)} %get-tuple-element.61) | copy-start | bytes 18436
  301.5 43.9 %copy-start.13 = (bf16[1,768,3,384]{1,3,2,0:T(8,128)(2,1)S(1)}, bf16[1,768,3,384]{1,3,2,0:T(8,128)(2,1)}, u32[]{:S(2)}) copy-start(bf16[1,768,3,384]{1,3,2,0:T(8,128)(2,1)} %copy.53) | copy-start | bytes 5308420
  301.5 392.5 %all-gather.9.cloned.1.call-start = ((), (), s32[]{:S(2)}) async-start(), calls=%async_computation.8 | async-start | bytes 2506752 | tf_op jit(solution)/shard_map/all_gather | solution.py:513
  336.6 401.1 %all-gather.11.cloned.1.call-start = ((), (), s32[]{:S(2)}) async-start(), calls=%async_computation.10 | async-start | bytes 2506752 | tf_op jit(solution)/shard_map/all_gather | solution.py:513
  465.6 108.7 %collective-permute-start.10 = (bf16[512,768]{1,0:T(8,128)(2,1)S(1)}, bf16[512,768]{1,0:T(8,128)(2,1)}, u32[]{:S(2)}, u32[]{:S(2)}) collective-permute-start(bf16[512,768]{1,0:T(8,128)(2,1)S(1)} %dynamic-slice_convert_fusion.1), channel_id=1, source_target_pairs={{0,1},{1,0},{2,3},{3,2},{4,5},{5,4},{6,7},{7,6},{8,9},{9,8},{10,11... | collective-permute-start | bytes 2359304 | tf_op jit(solution)/shard_map/ppermute | solution.py:389
  467.2 108.8 %collective-permute-start.11 = (bf16[512,768]{1,0:T(8,128)(2,1)S(1)}, bf16[512,768]{1,0:T(8,128)(2,1)}, u32[]{:S(2)}, u32[]{:S(2)}) collective-permute-start(bf16[512,768]{1,0:T(8,128)(2,1)S(1)} %dynamic-slice_convert_fusion), channel_id=1, source_target_pairs={{0,1},{1,0},{2,3},{3,2},{4,5},{5,4},{6,7},{7,6},{8,9},{9,8},{10,11... | collective-permute-start | bytes 2359304 | tf_op jit(solution)/shard_map/ppermute | solution.py:389
  535.3 44.1 %collective-permute-start.8 = (bf16[512,768]{1,0:T(8,128)(2,1)}, bf16[512,768]{1,0:T(8,128)(2,1)S(1)}, u32[]{:S(2)}, u32[]{:S(2)}) collective-permute-start(bf16[512,768]{1,0:T(8,128)(2,1)} %dynamic-slice_convert_fusion.2), channel_id=1, source_target_pairs={{0,1},{1,0},{2,3},{3,2},{4,5},{5,4},{6,7},{7,6},{8,9},{9,8},{10,11... | collective-permute-start | bytes 2359304 | tf_op jit(solution)/shard_map/ppermute | solution.py:389
  694.0 47.9 %copy-start.1 = (bf16[4,384,768]{2,1,0:T(8,128)(2,1)S(1)}, bf16[4,384,768]{2,1,0:T(8,128)(2,1)}, u32[]{:S(2)}) copy-start(bf16[4,384,768]{2,1,0:T(8,128)(2,1)} %param.25) | copy-start | bytes 7077892
  (45 other events, 362.7 us)
Sparse Core Ops, SparseCore 0:
  16.7 43.7 all-gather.4
  78.5 45.4 all-gather.6
  232.2 104.3 reduce-scatter.5
  343.4 106.1 reduce-scatter.7
  455.1 95.2 reduce-scatter.3
  553.7 96.4 all-reduce.2
  652.7 41.2 all-gather.8
  696.6 41.0 all-gather.10
